TPU v7x, 256 devices: a whole 4x4x8 slice. The times are simulated.
256 devices in a mesh: space: 32 (over x_hi, z, core), vel: 8 (over y, x_lo).
Axes of the slice: x: 4 (x_hi: 2, x_lo: 2; x = x_hi * 2 + x_lo), y: 4, z: 8, core: 2. Of those that a mesh axis runs over, the one named last changes fastest.
Arguments:
- dist: float32 [128, 8, 8, 4096], P('space', None, None, 'vel'), may hold values from 0 to 5.5, as said below
- cell_type: int32 [128, 8, 8], replicated, may hold values from 0 to 3, as said below
- boundary: float32 [6], replicated, may hold values from 0.8 to 1.2
Outputs:
- renewed: float32 [128, 8, 8, 4096], P('space', None, None, 'vel')
Inputs may be any that keep to these rules, and one draw needn't show every extreme that they name: `dist`: every entry is positive. `cell_type`: cells of kind 1 never lie on the grid's outer layer; kind 2 lies only in the plane x = 0 and kind 3 only in the plane x = 127, and both occur in every draw.
All inputs are finite; a program needn't handle non-finite values.
Results may differ from a plain program's by a relative error of at most 0.0003.
Values sent between devices are 32-bit elements; how exact they have to be, the bound alone decides.
A program may use at most 64 MiB of HBM per device.

v0:
```python
import functools
import math

import jax
import jax.numpy as jnp
from jax import lax
from jax.experimental import pallas as pl
from jax.experimental.pallas import tpu as pltpu
from jax.sharding import PartitionSpec as P

MESH = pl.DeviceIdType.MESH
F32 = jnp.float32
BF16 = jnp.bfloat16

NODES = 16
STEPS = 2
PRANDTL = 2.0 / 3.0
DT = 0.1
HALF = 0.05
VMAX = 5.0
KAPPA = VMAX / NODES
WEIGHT = (2.0 * VMAX / NODES) ** 3 / (2.0 * math.pi) ** 1.5
LOG2E = math.log2(math.e)
LN_KAPPA2 = 2.0 * math.log(KAPPA)
TILES = 4
LANES = 128


def minmod(a, b):
    return jnp.maximum(jnp.minimum(a, b), 0.0) + jnp.minimum(jnp.maximum(a, b), 0.0)


def put_rows(c_ref, n, base, rows):
    for i, r in enumerate(rows):
        c_ref[base + i : base + i + 1, :n] = r


def expansion(c_ref, n, l_ref):
    c = c_ref[:, :n]
    hi = c.astype(BF16).astype(F32)
    rest = c - hi
    mid = rest.astype(BF16).astype(F32)
    low = rest - mid
    full = jnp.concatenate([hi, mid, low, jnp.zeros((8, n), F32)], axis=0)
    l_ref[:n, :] = full.T


def gauss_rows(nu, speed_sq, inv_theta):
    zero = jnp.zeros_like(inv_theta)
    c4 = (-0.5 * LOG2E) * inv_theta
    c1 = LOG2E * inv_theta
    return [c4 * speed_sq, c1 * nu[0], c1 * nu[1], c1 * nu[2], c4, c4, c4]


def target_rows(tot_ref, n, c_ref, width, cells):
    row = lambda i: tot_ref[i : i + 1, :n]
    m0 = row(0)
    inv = 1.0 / m0
    nu = [row(1) * inv, row(2) * inv, row(3) * inv]
    speed_sq = nu[0] * nu[0] + nu[1] * nu[1] + nu[2] * nu[2]
    sxx, syy, szz, sxy, sxz, syz = (row(i) for i in range(4, 10))
    trace = sxx + syy + szz
    theta = (trace * inv - speed_sq) * (1.0 / 3.0)
    inv_theta = 1.0 / theta
    dots = (
        sxx * nu[0] + sxy * nu[1] + sxz * nu[2],
        sxy * nu[0] + syy * nu[1] + syz * nu[2],
        sxz * nu[0] + syz * nu[1] + szz * nu[2],
    )
    density = WEIGHT * m0
    tau2 = 0.2 * jnp.exp(-0.19 * (jnp.log(theta) + LN_KAPPA2)) / density
    damp = tau2 / (tau2 + width * PRANDTL)
    scale = damp * inv * inv_theta * inv_theta * (1.0 / 30.0)
    heat = [
        scale
        * (
            row(10 + i)
            + row(13 + i)
            - 2.0 * dots[i]
            - nu[i] * trace
            + 2.0 * m0 * nu[i] * speed_sq
        )
        for i in range(3)
    ]
    if cells:
        spread = 1.0 / (tau2 + DT)
        keep = (tau2 - HALF) * spread
        give = (3.0 * HALF) * spread
    else:
        spread = 1.0 / (tau2 + HALF)
        keep = tau2 * spread
        give = HALF * spread
    amp = give * density * inv_theta * jnp.sqrt(inv_theta) * (KAPPA**-3)
    drift = heat[0] * nu[0] + heat[1] * nu[1] + heat[2] * nu[2]
    excess = speed_sq * inv_theta - 5.0
    ah = [amp * h for h in heat]
    ai = amp * inv_theta
    dt = ai * drift
    aih = [ai * h for h in heat]
    ae = excess
    put_rows(c_ref, n, 0, gauss_rows(nu, speed_sq, inv_theta))
    put_rows(
        c_ref,
        n,
        16,
        [
            amp - amp * drift * excess,
            ah[0] * ae + 2.0 * dt * nu[0],
            ah[1] * ae + 2.0 * dt * nu[1],
            ah[2] * ae + 2.0 * dt * nu[2],
            -2.0 * aih[0] * nu[0] - dt,
            -2.0 * aih[1] * nu[1] - dt,
            -2.0 * aih[2] * nu[2] - dt,
            -2.0 * (aih[0] * nu[1] + aih[1] * nu[0]),
            -2.0 * (aih[0] * nu[2] + aih[2] * nu[0]),
            -2.0 * (aih[1] * nu[2] + aih[2] * nu[1]),
            aih[0],
            aih[1],
            aih[2],
            aih[0],
            aih[1],
            aih[2],
            keep,
        ],
    )


def solid_rows(tot_ref, kind, bound, c_ref, n):
    row = lambda i: tot_ref[i : i + 1, 128 : 128 + n]
    m0 = row(0)
    inv = 1.0 / m0
    zero = jnp.zeros_like(m0)
    inlet, outlet = kind == 2.0, kind == 3.0
    density = jnp.where(inlet, bound(0) + zero, jnp.where(outlet, bound(3) + zero, WEIGHT * m0))
    temper = jnp.where(inlet, bound(2) + zero, jnp.where(outlet, bound(4) + zero, bound(5) + zero))
    nu = [
        jnp.where(
            inlet,
            (bound(1) * (1.0 / KAPPA) if i == 0 else 0.0) + zero,
            jnp.where(outlet, row(1 + i) * inv, zero),
        )
        for i in range(3)
    ]
    speed_sq = nu[0] * nu[0] + nu[1] * nu[1] + nu[2] * nu[2]
    inv_t = 1.0 / temper
    put_rows(c_ref, n, 0, gauss_rows(nu, speed_sq, inv_t * (KAPPA * KAPPA)))
    put_rows(c_ref, n, 32, [density * inv_t * jnp.sqrt(inv_t)])


def kernel(
    n_space,
    n_vel,
    dist,
    kinds,
    bound_ref,
    out,
    F,
    B,
    X,
    Y,
    Z,
    W,
    MX,
    Sc,
    Rc,
    Rl,
    Rr,
    Sf,
    Rf,
    tot,
    C,
    CM,
    Lc,
    Lm,
    Lf,
    TE,
    TP,
    TA,
    T16,
    kt,
    kb,
    kr,
    in_sem,
    kt_sem,
    halo_s,
    halo_r,
    cell_s,
    cell_r,
    left_s,
    left_r,
    right_s,
    right_r,
    face_s,
    face_r,
):
    s = lax.axis_index("space")
    v = lax.axis_index("vel")
    positive = v >= n_vel // 2
    last = n_space - 1
    total_planes = 4 * n_space
    bound = lambda i: bound_ref[i]
    place = lambda q: jnp.where(positive, q, 7 - q)

    load = pltpu.make_async_copy(dist, F.at[0, 2:6], in_sem)
    load.start()
    kind_loads = []
    for j in range(6):
        plane = jnp.clip(4 * s + (j - 1), 0, total_planes - 1)
        cp = pltpu.make_async_copy(kinds.at[plane], kt.at[j], kt_sem.at[j])
        cp.start()
        kind_loads.append(cp)

    barrier = pltpu.get_barrier_semaphore()
    for d in range(1, n_vel):
        pl.semaphore_signal(
            barrier, 1, device_id={"vel": lax.rem(v + d, n_vel)}, device_id_type=MESH
        )

    def greet(to):
        for d in range(n_vel):
            pl.semaphore_signal(
                barrier,
                1,
                device_id={"space": to, "vel": lax.rem(v + d, n_vel)},
                device_id_type=MESH,
            )

    pl.when(s > 0)(lambda: greet(s - 1))
    pl.when(s < last)(lambda: greet(s + 1))

    node = lax.broadcasted_iota(jnp.int32, (1, TILES * LANES), 1)
    nx = (4 * v - 15 + 2 * (node // 256)).astype(F32)
    ny = (2 * (node // 16 % 16) - 15).astype(F32)
    nz = (2 * (node % 16) - 15).astype(F32)
    square = nx * nx + ny * ny + nz * nz
    cubes = [nx * square, ny * square, nz * square]
    coarse = [c.astype(BF16).astype(F32) for c in cubes]
    rows = [jnp.ones_like(nx), nx, ny, nz, nx * nx, ny * ny, nz * nz, nx * ny, nx * nz, ny * nz]
    rows += coarse + [c - h for c, h in zip(cubes, coarse)]
    table = jnp.concatenate(rows, axis=0)
    z8 = jnp.zeros((8, TILES * LANES), F32)
    T16[...] = table.astype(BF16)
    TE[...] = jnp.concatenate([table, z8, z8, z8] * 3 + [z8], axis=0).astype(BF16)
    TP[...] = jnp.concatenate([z8, z8, table, z8] * 3 + [z8], axis=0).astype(BF16)
    line = lax.broadcasted_iota(jnp.int32, (128, LANES), 0)
    TA[...] = jnp.where(line % 40 == 32, 1.0, 0.0).astype(BF16)
    C[...] = jnp.zeros_like(C)
    CM[...] = jnp.zeros_like(CM)

    lane = lax.broadcasted_iota(jnp.int32, (8, LANES), 1)
    sub = lax.broadcasted_iota(jnp.int32, (8, LANES), 0)
    xi_x = [KAPPA * (4 * v - 15 + 2 * a).astype(F32) for a in range(2)]
    abs_x = [jnp.abs(x) for x in xi_x]
    xi_y = [KAPPA * (2 * (lane // 16 + 8 * b) - 15).astype(F32) for b in range(2)]
    xi_z = KAPPA * (2 * (lane % 16) - 15).astype(F32)
    up_z = lane % 16 >= 8

    def moments(values, cells):
        hi = values.astype(BF16)
        low = (values - hi.astype(F32)).astype(BF16)
        nt = (((1,), (1,)), ((), ()))
        t = T16[...]
        return lax.dot_general(t, hi, nt, preferred_element_type=F32) + lax.dot_general(
            t, low, nt, preferred_element_type=F32
        )

    def relax(l_rows, get, put):
        left = l_rows.astype(BF16)
        e = jnp.dot(left, TE[...], preferred_element_type=F32)
        p = jnp.dot(left, TP[...], preferred_element_type=F32)
        a = jnp.dot(left, TA[...], preferred_element_type=F32)
        for t in range(TILES):
            cut = slice(t * LANES, (t + 1) * LANES)
            put(t, a * get(t) + jnp.exp2(e[:, cut]) * p[:, cut])

    def peer_copies(src, dst, send, recv, lo, extra):
        return [
            pltpu.make_async_remote_copy(
                src,
                dst.at[d - lo],
                send.at[d - lo],
                recv.at[d - lo],
                device_id={**extra, "vel": lax.rem(v + d, n_vel)},
                device_id_type=MESH,
            )
            for d in range(lo, n_vel)
        ]

    def cell_copies(k):
        return peer_copies(Sc.at[k], Rc.at[k], cell_s.at[k], cell_r.at[k], 1, {})

    def right_copies(k):
        return peer_copies(
            Sc.at[k, :, 128:256], Rl.at[k], right_s.at[k], left_r.at[k], 0, {"space": s + 1}
        )

    def left_copies(k):
        return peer_copies(
            Sc.at[k, :, 0:128], Rr.at[k], left_s.at[k], right_r.at[k], 0, {"space": s - 1}
        )

    down = jnp.where(positive, s + 1, s - 1)
    upw = jnp.where(positive, s - 1, s + 1)
    has_down = jnp.where(positive, s < last, s > 0)
    has_up = jnp.where(positive, s > 0, s < last)

    def down_copies(k):
        near_src, far_src = place(5), place(4)
        near_dst, far_dst = place(1), place(0)
        return [
            pltpu.make_async_remote_copy(
                F.at[k, near_src],
                F.at[k, near_dst],
                halo_s.at[k, 0],
                halo_r.at[k, 0],
                device_id={"space": down},
                device_id_type=MESH,
            ),
            pltpu.make_async_remote_copy(
                F.at[k, far_src, 1:7],
                F.at[k, far_dst, 1:7],
                halo_s.at[k, 1],
                halo_r.at[k, 1],
                device_id={"space": down},
                device_id_type=MESH,
            ),
        ]

    def up_copies(k):
        return [
            pltpu.make_async_remote_copy(
                F.at[k, place(2), 1:7],
                F.at[k, place(6), 1:7],
                halo_s.at[k, 2],
                halo_r.at[k, 2],
                device_id={"space": upw},
                device_id_type=MESH,
            )
        ]

    def start(copies):
        for cp in copies:
            cp.start()

    def landed(copies):
        for cp in copies:
            cp.wait_recv()

    def left_free(copies):
        for cp in copies:
            cp.wait_send()

    def send_cells(k):
        start(cell_copies(k))
        pl.when(s < last)(lambda: start(right_copies(k)))
        pl.when(s > 0)(lambda: start(left_copies(k)))

    def send_halo(k):
        pl.when(has_down)(lambda: start(down_copies(k)))
        pl.when(has_up)(lambda: start(up_copies(k)))

    def face_copies(k, e):
        return peer_copies(Sf.at[k, e], Rf.at[k, e], face_s.at[k, e], face_r.at[k, e], 1, {})

    load.wait()
    Sc[0] = moments(F[0, 2:6].reshape(256, TILES * LANES), 256)

    inside = (s > 0) & (s < last)
    pl.when(inside)(lambda: pl.semaphore_wait(barrier, 3 * n_vel - 1))
    pl.when(jnp.logical_not(inside))(lambda: pl.semaphore_wait(barrier, 2 * n_vel - 1))
    send_halo(0)
    send_cells(0)

    for cp in kind_loads:
        cp.wait()
    tile8 = lax.broadcasted_iota(jnp.int32, (8, 8), 0) == lax.broadcasted_iota(
        jnp.int32, (8, 8), 1
    )
    for j in range(6):
        for y in range(8):
            line8 = jnp.broadcast_to(kt[j, y : y + 1, :].astype(F32), (8, 8))
            column = jnp.sum(jnp.where(tile8, line8, 0.0), axis=1, keepdims=True)
            kb[j, y] = jnp.broadcast_to(column, (8, LANES))
    for pair in range(2):
        gathered = jnp.zeros((8, LANES), F32)
        for half in range(2):
            for y in range(8):
                here = lane // 8 == half * 8 + y
                gathered = jnp.where(here, kb[1 + 2 * pair + half, y], gathered)
        gathered = jnp.where(lane % 8 == sub, gathered, 0.0)
        kr[0:1, pair * LANES : (pair + 1) * LANES] = jnp.sum(gathered, axis=0, keepdims=True)
    for j in range(6):
        for y in range(8):
            kb[j, y] = jnp.where(kb[j, y] == 1.0, 1.0, 0.0)

    def one_step(k):
        landed(cell_copies(k))
        sums = Sc[k]
        for d in range(n_vel - 1):
            sums = sums + Rc[k, d]
        tot[:, 128:384] = sums

        def from_left():
            landed(right_copies(k))
            part = Rl[k, 0]
            for d in range(1, n_vel):
                part = part + Rl[k, d]
            tot[:, 0:128] = part

        def from_right():
            landed(left_copies(k))
            part = Rr[k, 0]
            for d in range(1, n_vel):
                part = part + Rr[k, d]
            tot[:, 384:512] = part

        def no_left():
            tot[:, 0:128] = tot[:, 128:256]

        def no_right():
            tot[:, 384:512] = tot[:, 256:384]

        pl.when(s > 0)(from_left)
        pl.when(s == 0)(no_left)
        pl.when(s < last)(from_right)
        pl.when(s == last)(no_right)
        target_rows(tot, 512, C, DT, True)
        expansion(C, 512, Lc)

        pl.when(has_up)(lambda: landed(down_copies(k)))
        pl.when(has_down)(lambda: landed(up_copies(k)))

        def no_up():
            F[k, place(0)] = F[k, place(2)]
            F[k, place(1)] = F[k, place(2)]

        def no_down():
            F[k, place(6)] = F[k, place(5)]

        pl.when(jnp.logical_not(has_up))(no_up)
        pl.when(jnp.logical_not(has_down))(no_down)

        def before(q, carry):
            i = place(q)
            l_rows = Lc[pl.ds(pl.multiple_of(i * 64, 64), 64), :]

            def get(t):
                return F[k, i, :, :, t * LANES : (t + 1) * LANES].reshape(64, LANES)

            def put(t, value):
                B[i, :, :, t * LANES : (t + 1) * LANES] = value.reshape(8, 8, LANES)

            relax(l_rows, get, put)
            return carry

        lax.fori_loop(0, 7, before, 0)

        def upwind(q, across):
            i, im, ip = place(q), place(q - 1), place(q + 1)
            face = jnp.where(positive, q - 1, 5 - q)
            own = i - 2
            for y in range(1, 7):
                fluid = kb[i - 1, y]
                for t in range(TILES):
                    cut = slice(t * LANES, (t + 1) * LANES)
                    b = B[i, y, :, cut]
                    slope_x = minmod(B[ip, y, :, cut] - b, b - B[im, y, :, cut]) * fluid
                    slope_y = minmod(B[i, y + 1, :, cut] - b, b - B[i, y - 1, :, cut]) * fluid
                    ahead = pltpu.roll(b, 7, 0) - b
                    slope_z = minmod(ahead, pltpu.roll(ahead, 1, 0)) * fluid
                    centre = b - HALF * (
                        abs_x[t // 2] * slope_x + xi_y[t % 2] * slope_y + xi_z * slope_z
                    )
                    X[face, y - 1, :, cut] = centre + 0.5 * slope_x
                    if across:
                        if t % 2:
                            Y[own, y, :, cut] = centre + 0.5 * slope_y
                        else:
                            Y[own, y - 1, :, cut] = centre - 0.5 * slope_y
                        edge = centre + jnp.where(up_z, 0.5 * slope_z, -0.5 * slope_z)
                        Z[own, y - 1, :, cut] = jnp.where(up_z, edge, pltpu.roll(edge, 7, 0))
            if across:
                for t in range(TILES):
                    cut = slice(t * LANES, (t + 1) * LANES)
                    if t % 2:
                        Y[own, 0, :, cut] = B[i, 0, :, cut]
                    else:
                        Y[own, 6, :, cut] = B[i, 7, :, cut]

        upwind(1, False)

        def upwind_own(q, carry):
            upwind(q, True)
            return carry

        lax.fori_loop(2, 6, upwind_own, 0)

        for e, (faces, count) in enumerate(((X, 240), (Y, 224), (Z, 192))):
            Sf[k, e, :, :count] = moments(faces[...].reshape(count, TILES * LANES), count)
            start(face_copies(k, e))

        solid_rows(tot, kr[0:1, :], bound, CM, 256)
        expansion(CM, 256, Lm)
        target = F.at[1, 2:6] if k == 0 else out

        def solids(p, carry):
            left = Lm[pl.ds(pl.multiple_of(p * 64, 64), 64), :].astype(BF16)
            e = jnp.dot(left, TE[...], preferred_element_type=F32)
            a = jnp.dot(left, TA[...], preferred_element_type=F32)
            for t in range(TILES):
                cut = slice(t * LANES, (t + 1) * LANES)
                target[p, :, :, cut] = (a * jnp.exp2(e[:, cut])).reshape(8, 8, LANES)
            W[p] = (4.0 * B[p + 2, 1:7] - F[k, p + 2, 1:7]) * (1.0 / 3.0)
            return carry

        lax.fori_loop(0, 4, solids, 0)

        for e, (faces, parts, lines) in enumerate(((X, 5, 6), (Y, 4, 7), (Z, 4, 6))):
            landed(face_copies(k, e))
            sums = Sf[k, e]
            for d in range(n_vel - 1):
                sums = sums + Rf[k, e, d]
            tot[:, 0:256] = sums
            target_rows(tot, 256, C, HALF, False)
            expansion(C, 256, Lf)
            size = lines * 8

            def flux(i, carry, faces=faces, lines=lines, size=size):
                l_rows = Lf[pl.ds(pl.multiple_of(i * size, 8), size), :]

                def get(t):
                    return faces[i, :, :, t * LANES : (t + 1) * LANES].reshape(size, LANES)

                def put(t, value):
                    faces[i, :, :, t * LANES : (t + 1) * LANES] = value.reshape(lines, 8, LANES)

                relax(l_rows, get, put)
                return carry

            lax.fori_loop(0, parts, flux, 0)

        def renew(p, carry):
            for y in range(1, 7):
                fluid = kb[p + 1, y] == 1.0
                for t in range(TILES):
                    cut = slice(t * LANES, (t + 1) * LANES)
                    z = Z[p, y - 1, :, cut]
                    change = (
                        xi_x[t // 2] * (X[p + 1, y - 1, :, cut] - X[p, y - 1, :, cut])
                        + xi_y[t % 2] * (Y[p, y, :, cut] - Y[p, y - 1, :, cut])
                        + xi_z * (z - pltpu.roll(z, 1, 0))
                    )
                    fresh = W[p, y - 1, :, cut] - DT * change
                    target[p, y, :, cut] = jnp.where(fluid, fresh, target[p, y, :, cut])
            return carry

        lax.fori_loop(0, 4, renew, 0)

    one_step(0)
    send_halo(1)
    Sc[1] = moments(F[1, 2:6].reshape(256, TILES * LANES), 256)
    send_cells(1)
    one_step(1)

    for k in range(STEPS):
        left_free(cell_copies(k))
        pl.when(s < last)(lambda k=k: left_free(right_copies(k)))
        pl.when(s > 0)(lambda k=k: left_free(left_copies(k)))
        pl.when(has_down)(lambda k=k: left_free(down_copies(k)))
        pl.when(has_up)(lambda k=k: left_free(up_copies(k)))
        for e in range(3):
            left_free(face_copies(k, e))


def solution(mesh):
    n_space, n_vel = mesh.shape["space"], mesh.shape["vel"]
    vmem, dma = pltpu.VMEM, pltpu.SemaphoreType.DMA
    width = TILES * LANES

    def on_device(dist, cell_type, boundary):
        peers = n_vel - 1
        return pl.pallas_call(
            functools.partial(kernel, n_space, n_vel),
            out_shape=jax.ShapeDtypeStruct(dist.shape, F32),
            in_specs=[
                pl.BlockSpec(memory_space=pl.ANY),
                pl.BlockSpec(memory_space=pl.ANY),
                pl.BlockSpec(memory_space=pltpu.SMEM),
            ],
            out_specs=pl.BlockSpec(memory_space=pltpu.VMEM),
            scratch_shapes=[
                vmem((2, 8, 8, 8, width), F32),
                vmem((8, 8, 8, width), F32),
                vmem((5, 6, 8, width), F32),
                vmem((4, 7, 8, width), F32),
                vmem((4, 6, 8, width), F32),
                vmem((4, 6, 8, width), F32),
                vmem((8, LANES), F32),
                vmem((2, 16, 256), F32),
                vmem((2, peers, 16, 256), F32),
                vmem((2, n_vel, 16, 128), F32),
                vmem((2, n_vel, 16, 128), F32),
                vmem((2, 3, 16, 256), F32),
                vmem((2, 3, peers, 16, 256), F32),
                vmem((16, 512), F32),
                vmem((40, 512), F32),
                vmem((40, 256), F32),
                vmem((512, 128), F32),
                vmem((256, 128), F32),
                vmem((256, 128), F32),
                vmem((128, width), BF16),
                vmem((128, width), BF16),
                vmem((128, LANES), BF16),
                vmem((16, width), BF16),
                vmem((6, 8, 8), jnp.int32),
                vmem((6, 8, 8, LANES), F32),
                vmem((8, 256), F32),
                dma,
                dma((6,)),
                dma((2, 3)),
                dma((2, 3)),
                dma((2, peers)),
                dma((2, peers)),
                dma((2, n_vel)),
                dma((2, n_vel)),
                dma((2, n_vel)),
                dma((2, n_vel)),
                dma((2, 3, peers)),
                dma((2, 3, peers)),
            ],
            compiler_params=pltpu.CompilerParams(
                collective_id=0, has_side_effects=True, vmem_limit_bytes=40 * 2**20
            ),
        )(dist, cell_type, boundary)

    return jax.shard_map(
        on_device,
        mesh=mesh,
        in_specs=(P("space", None, None, "vel"), P(), P()),
        out_specs=P("space", None, None, "vel"),
        check_vma=False,
    )
```

profile of v0, /device:TPU:4, one launch (start us, length us, event | category | flops | bytes accessed | tf_op | source)
XLA Modules:
  0.0 48.8 jit_solution(5337436864925875991)
XLA Ops:
  0.0 0.0 copy-start.1
  0.0 0.0 copy-start
  0.0 1.1 %copy.4.kinds = s32[128,8,8]{2,1,0:T(8,128)S(1)} copy(s32[128,8,8]{0,2,1:T(8,128)} %param.4) | data formatting | bytes 65536 | tf_op args[1]
  1.1 0.0 copy-done.1
  1.1 0.0 copy-done
  1.1 46.9 %shard_map.37 = f32[4,8,8,512]{3,2,1,0:T(8,128)S(1)} custom-call(f32[4,8,8,512]{3,2,1,0:T(8,128)S(1)} %copy-done, s32[128,8,8]{2,1,0:T(8,128)S(1)} %copy.4.kinds, f32[6]{0:T(128)S(1)} %copy-done.1), custom_call_target="tpu_custom_call" | custom-call | tf_op jit(solution)/shard_map/pallas_call | solution.py:582
  48.0 0.8 %copy.6 = f32[4,8,8,512]{3,2,1,0:T(8,128)} copy(f32[4,8,8,512]{3,2,1,0:T(8,128)S(1)} %shard_map.37) | data formatting | bytes 1048576
Async XLA Ops:
  0.0 1.1 %copy-start.1 = (f32[6]{0:T(128)S(1)}, f32[6]{0:T(128)}, u32[]{:S(2)}) copy-start(f32[6]{0:T(128)} %bound_ref.1) | copy-start | bytes 76
  0.0 1.1 %copy-start = (f32[4,8,8,512]{3,2,1,0:T(8,128)S(1)}, f32[4,8,8,512]{3,2,1,0:T(8,128)}, u32[]{:S(2)}) copy-start(f32[4,8,8,512]{3,2,1,0:T(8,128)} %dist.1) | copy-start | bytes 1572868
where the time goes:
time: 48.8 us
  Pallas kernels  46.9 us (96%)
  local copies, waits for them, and re-layouts  1.85 us (4%)
    pallas_call x1, Pallas kernels, on_device(): pl.pallas_call(functools.partial(kernel, n_space, n_vel), out_shape=jax.S...  46.9 us
    unnamed x6, local copies, waits for them, and re-layouts  1.85 us

commit v1 on v0

v1 whole, which is shorter than its diff:
```python
import functools
import math

import jax
import jax.numpy as jnp
from jax import lax
from jax.experimental import pallas as pl
from jax.experimental.pallas import tpu as pltpu
from jax.sharding import PartitionSpec as P

MESH = pl.DeviceIdType.MESH
F32 = jnp.float32
BF16 = jnp.bfloat16

NODES = 16
STEPS = 2
PRANDTL = 2.0 / 3.0
DT = 0.1
HALF = 0.05
VMAX = 5.0
KAPPA = VMAX / NODES
WEIGHT = (2.0 * VMAX / NODES) ** 3 / (2.0 * math.pi) ** 1.5
LOG2E = math.log2(math.e)
LN_KAPPA2 = 2.0 * math.log(KAPPA)
TILES = 4
LANES = 128

X_AT = (32, 38, 0, 44, 50)
Y_AT = (56, 6, 13, 63)
Z_AT = (70, 20, 26, 76)
INNER = 32
FACES = 82


def minmod(a, b):
    return jnp.maximum(jnp.minimum(a, b), 0.0) + jnp.minimum(jnp.maximum(a, b), 0.0)


def put_rows(c_ref, n, base, rows):
    for i, r in enumerate(rows):
        c_ref[base + i : base + i + 1, :n] = r


def expansion(c_ref, n, l_ref):
    c = c_ref[:, :n]
    hi = c.astype(BF16).astype(F32)
    rest = c - hi
    mid = rest.astype(BF16).astype(F32)
    low = rest - mid
    full = jnp.concatenate([hi, mid, low, jnp.zeros((8, n), F32)], axis=0)
    l_ref[:n, :] = full.T


def gauss_rows(nu, speed_sq, inv_theta):
    zero = jnp.zeros_like(inv_theta)
    c4 = (-0.5 * LOG2E) * inv_theta
    c1 = LOG2E * inv_theta
    return [c4 * speed_sq, c1 * nu[0], c1 * nu[1], c1 * nu[2], c4, c4, c4]


def target_rows(tot_ref, n, c_ref, width, cells):
    row = lambda i: tot_ref[i : i + 1, :n]
    m0 = row(0)
    inv = 1.0 / m0
    nu = [row(1) * inv, row(2) * inv, row(3) * inv]
    speed_sq = nu[0] * nu[0] + nu[1] * nu[1] + nu[2] * nu[2]
    sxx, syy, szz, sxy, sxz, syz = (row(i) for i in range(4, 10))
    trace = sxx + syy + szz
    theta = (trace * inv - speed_sq) * (1.0 / 3.0)
    inv_theta = 1.0 / theta
    dots = (
        sxx * nu[0] + sxy * nu[1] + sxz * nu[2],
        sxy * nu[0] + syy * nu[1] + syz * nu[2],
        sxz * nu[0] + syz * nu[1] + szz * nu[2],
    )
    density = WEIGHT * m0
    tau2 = 0.2 * jnp.exp(-0.19 * (jnp.log(theta) + LN_KAPPA2)) / density
    damp = tau2 / (tau2 + width * PRANDTL)
    scale = damp * inv * inv_theta * inv_theta * (1.0 / 30.0)
    heat = [
        scale
        * (
            row(10 + i)
            - 2.0 * dots[i]
            - nu[i] * trace
            + 2.0 * m0 * nu[i] * speed_sq
        )
        for i in range(3)
    ]
    if cells:
        spread = 1.0 / (tau2 + DT)
        keep = (tau2 - HALF) * spread
        give = (3.0 * HALF) * spread
    else:
        spread = 1.0 / (tau2 + HALF)
        keep = tau2 * spread
        give = HALF * spread
    amp = give * density * inv_theta * jnp.sqrt(inv_theta) * (KAPPA**-3)
    drift = heat[0] * nu[0] + heat[1] * nu[1] + heat[2] * nu[2]
    excess = speed_sq * inv_theta - 5.0
    ah = [amp * h for h in heat]
    ai = amp * inv_theta
    dt = ai * drift
    aih = [ai * h for h in heat]
    ae = excess
    put_rows(c_ref, n, 0, gauss_rows(nu, speed_sq, inv_theta))
    put_rows(
        c_ref,
        n,
        16,
        [
            amp - amp * drift * excess,
            ah[0] * ae + 2.0 * dt * nu[0],
            ah[1] * ae + 2.0 * dt * nu[1],
            ah[2] * ae + 2.0 * dt * nu[2],
            -2.0 * aih[0] * nu[0] - dt,
            -2.0 * aih[1] * nu[1] - dt,
            -2.0 * aih[2] * nu[2] - dt,
            -2.0 * (aih[0] * nu[1] + aih[1] * nu[0]),
            -2.0 * (aih[0] * nu[2] + aih[2] * nu[0]),
            -2.0 * (aih[1] * nu[2] + aih[2] * nu[1]),
            aih[0],
            aih[1],
            aih[2],
            aih[0],
            aih[1],
            aih[2],
            keep,
        ],
    )


def solid_rows(tot_ref, kind, bound, c_ref, n):
    row = lambda i: tot_ref[i : i + 1, :n]
    m0 = row(0)
    inv = 1.0 / m0
    zero = jnp.zeros_like(m0)
    inlet, outlet = kind == 2.0, kind == 3.0
    density = jnp.where(inlet, bound(0) + zero, jnp.where(outlet, bound(3) + zero, WEIGHT * m0))
    temper = jnp.where(inlet, bound(2) + zero, jnp.where(outlet, bound(4) + zero, bound(5) + zero))
    nu = [
        jnp.where(
            inlet,
            (bound(1) * (1.0 / KAPPA) if i == 0 else 0.0) + zero,
            jnp.where(outlet, row(1 + i) * inv, zero),
        )
        for i in range(3)
    ]
    speed_sq = nu[0] * nu[0] + nu[1] * nu[1] + nu[2] * nu[2]
    inv_t = 1.0 / temper
    put_rows(c_ref, n, 0, gauss_rows(nu, speed_sq, inv_t * (KAPPA * KAPPA)))
    put_rows(c_ref, n, 32, [density * inv_t * jnp.sqrt(inv_t)])


def kernel(
    n_space,
    n_vel,
    dist,
    kinds,
    bound_ref,
    out,
    F,
    B,
    G,
    W,
    O,
    Sc,
    Rc,
    Rl,
    Rr,
    Sf1,
    Rf1,
    Sf2,
    Rf2,
    totc,
    tote,
    totf,
    C,
    CM,
    Lc,
    Le,
    Lm,
    Lf,
    TE,
    TP,
    TA,
    T32,
    kt,
    kb,
    kr,
    in_sem,
    kt_sem,
    out_sem,
    halo_s,
    halo_r,
    cell_s,
    cell_r,
    left_s,
    left_r,
    right_s,
    right_r,
    face_s,
    face_r,
):
    s = lax.axis_index("space")
    v = lax.axis_index("vel")
    positive = v >= n_vel // 2
    last = n_space - 1
    bound = lambda i: bound_ref[i]
    place = lambda q: jnp.where(positive, q, 7 - q)

    barrier = pltpu.get_barrier_semaphore()
    for d in range(1, n_vel):
        pl.semaphore_signal(
            barrier, 1, device_id={"vel": lax.rem(v + d, n_vel)}, device_id_type=MESH
        )

    def greet(to):
        pl.semaphore_signal(barrier, 1, device_id={"space": to}, device_id_type=MESH)

    pl.when(s > 0)(lambda: greet(s - 1))
    pl.when(s < last)(lambda: greet(s + 1))

    load = pltpu.make_async_copy(dist, F.at[0, 2:6], in_sem)
    load.start()
    kind_load = pltpu.make_async_copy(kinds, kt, kt_sem)
    kind_load.start()

    node = lax.broadcasted_iota(jnp.int32, (1, TILES * LANES), 1)
    nx = (4 * v - 15 + 2 * (node // 256)).astype(F32)
    ny = (2 * (node // 16 % 16) - 15).astype(F32)
    nz = (2 * (node % 16) - 15).astype(F32)
    square = nx * nx + ny * ny + nz * nz
    cubes = [nx * square, ny * square, nz * square]
    coarse = [c.astype(BF16).astype(F32) for c in cubes]
    rows = [jnp.ones_like(nx), nx, ny, nz, nx * nx, ny * ny, nz * nz, nx * ny, nx * nz, ny * nz]
    rows += coarse + [c - h for c, h in zip(cubes, coarse)]
    table = jnp.concatenate(rows, axis=0)
    z8 = jnp.zeros((8, TILES * LANES), F32)
    z3 = jnp.zeros((3, TILES * LANES), F32)
    T32[...] = jnp.concatenate(
        rows[:13] + [z3, jnp.zeros((10, TILES * LANES), F32)] + rows[13:] + [z3], axis=0
    ).astype(BF16)
    TE[...] = jnp.concatenate([table, z8, z8, z8] * 3 + [z8], axis=0).astype(BF16)
    TP[...] = jnp.concatenate([z8, z8, table, z8] * 3 + [z8], axis=0).astype(BF16)
    line = lax.broadcasted_iota(jnp.int32, (128, LANES), 0)
    TA[...] = jnp.where(line % 40 == 32, 1.0, 0.0).astype(BF16)
    C[...] = jnp.zeros_like(C)
    CM[...] = jnp.zeros_like(CM)

    lane = lax.broadcasted_iota(jnp.int32, (8, LANES), 1)
    sub = lax.broadcasted_iota(jnp.int32, (8, LANES), 0)
    xi_x = [KAPPA * (4 * v - 15 + 2 * a).astype(F32) for a in range(2)]
    abs_x = [jnp.abs(x) for x in xi_x]
    xi_y = [KAPPA * (2 * (lane // 16 + 8 * b) - 15).astype(F32) for b in range(2)]
    xi_z = KAPPA * (2 * (lane % 16) - 15).astype(F32)
    up_z = lane % 16 >= 8

    def moments(values):
        hi = values.astype(BF16)
        low = (values - hi.astype(F32)).astype(BF16)
        nt = (((1,), (1,)), ((), ()))
        t = T32[...]
        both = lax.dot_general(t, hi, nt, preferred_element_type=F32) + lax.dot_general(
            t, low, nt, preferred_element_type=F32
        )
        return both[0:16] + both[16:32]

    def relax(l_rows, get, put):
        left = l_rows.astype(BF16)
        e = jnp.dot(left, TE[...], preferred_element_type=F32)
        p = jnp.dot(left, TP[...], preferred_element_type=F32)
        a = jnp.dot(left, TA[...], preferred_element_type=F32)
        for t in range(TILES):
            cut = slice(t * LANES, (t + 1) * LANES)
            put(t, a * get(t) + jnp.exp2(e[:, cut]) * p[:, cut])

    def peer_copies(src, dst, send, recv, lo, extra):
        return [
            pltpu.make_async_remote_copy(
                src,
                dst.at[d - lo],
                send.at[d - lo],
                recv.at[d - lo],
                device_id={**extra, "vel": lax.rem(v + d, n_vel)},
                device_id_type=MESH,
            )
            for d in range(lo, n_vel)
        ]

    def cell_copies(k):
        return peer_copies(
            Sc.at[k], Rc.at[k], cell_s.at[k], cell_r.at[k], 1, {}
        )

    def edge_copies(k, src, dst, send, recv, to):
        return [
            pltpu.make_async_remote_copy(
                totc.at[k, :, src],
                dst.at[k],
                send.at[k],
                recv.at[k],
                device_id=to,
                device_id_type=MESH,
            )
        ]

    def right_copies(k):
        return edge_copies(k, slice(128, 256), Rl, right_s, left_r, {"space": s + 1})

    def left_copies(k):
        return edge_copies(k, slice(0, 128), Rr, left_s, right_r, {"space": s - 1})

    down = jnp.where(positive, s + 1, s - 1)
    upw = jnp.where(positive, s - 1, s + 1)
    has_down = jnp.where(positive, s < last, s > 0)
    has_up = jnp.where(positive, s > 0, s < last)

    def halo_copy(k, which, src, dst, to):
        return pltpu.make_async_remote_copy(
            src,
            dst,
            halo_s.at[k, which],
            halo_r.at[k, which],
            device_id={"space": to},
            device_id_type=MESH,
        )

    def near_copies(k):
        return [halo_copy(k, 0, F.at[k, place(5)], F.at[k, place(1)], down)]

    def far_copies(k):
        return [halo_copy(k, 1, F.at[k, place(4), 1:7], F.at[k, place(0), 1:7], down)]

    def up_copies(k):
        return [halo_copy(k, 2, F.at[k, place(2), 1:7], F.at[k, place(6), 1:7], upw)]

    def start(copies):
        for cp in copies:
            cp.start()

    def landed(copies):
        for cp in copies:
            cp.wait_recv()

    def left_free(copies):
        for cp in copies:
            cp.wait_send()

    def send_edges(k):
        pl.when(s < last)(lambda: start(right_copies(k)))
        pl.when(s > 0)(lambda: start(left_copies(k)))

    def send_cells(k):
        Sc[k] = moments(F[k, 2:6].reshape(256, TILES * LANES))
        start(cell_copies(k))

    def send_near(k):
        pl.when(has_down)(lambda: start(near_copies(k)))
        pl.when(has_up)(lambda: start(up_copies(k)))

    def send_far(k):
        pl.when(has_down)(lambda: start(far_copies(k)))

    def face_copies(k, g):
        sf, rf = ((Sf1, Rf1), (Sf2, Rf2))[g]
        return peer_copies(
            sf.at[k], rf.at[k], face_s.at[k, g], face_r.at[k, g], 1, {}
        )

    load.wait()
    Sc[0] = moments(F[0, 2:6].reshape(256, TILES * LANES))

    inside = (s > 0) & (s < last)
    pl.when(inside)(lambda: pl.semaphore_wait(barrier, n_vel + 1))
    pl.when(jnp.logical_not(inside))(lambda: pl.semaphore_wait(barrier, n_vel))
    start(cell_copies(0))
    send_near(0)
    send_far(0)

    kind_load.wait()
    for j in range(6):
        plane = 4 * s + (j - 1)
        for y in range(8):
            column = jnp.sum(
                jnp.where(lane == plane, kt[y], 0).astype(F32), axis=1, keepdims=True
            )
            kb[j, y] = jnp.broadcast_to(column, (8, LANES))
    for pair in range(2):
        gathered = jnp.zeros((8, LANES), F32)
        for half in range(2):
            for y in range(8):
                here = lane // 8 == half * 8 + y
                gathered = jnp.where(here, kb[1 + 2 * pair + half, y], gathered)
        gathered = jnp.where(lane % 8 == sub, gathered, 0.0)
        kr[0:1, pair * LANES : (pair + 1) * LANES] = jnp.sum(gathered, axis=0, keepdims=True)
    for j in range(6):
        for y in range(8):
            kb[j, y] = jnp.where(kb[j, y] == 1.0, 1.0, 0.0)

    def one_step(k):
        def before(i, l_rows):
            def get(t):
                return F[k, i, :, :, t * LANES : (t + 1) * LANES].reshape(64, LANES)

            def put(t, value):
                B[i, :, :, t * LANES : (t + 1) * LANES] = value.reshape(8, 8, LANES)

            relax(l_rows, get, put)

        landed(cell_copies(k))
        sums = Sc[k]
        for d in range(n_vel - 1):
            sums = sums + Rc[k, d]
        totc[k] = sums
        send_edges(k)
        target_rows(totc.at[k], 256, C, DT, True)
        expansion(C, 256, Lc)
        for i in range(4):
            before(i + 2, Lc[i * 64 : i * 64 + 64, :])

        def upwind(q, across):
            i, im, ip = place(q), place(q - 1), place(q + 1)
            pick = lambda table: jnp.where(positive, table[0], table[1])
            x_at = pick((X_AT[q - 1], X_AT[5 - q]))
            if across:
                y_at = pick((Y_AT[q - 2], Y_AT[5 - q]))
                z_at = pick((Z_AT[q - 2], Z_AT[5 - q]))
            for y in range(1, 7):
                fluid = kb[i - 1, y]
                for t in range(TILES):
                    cut = slice(t * LANES, (t + 1) * LANES)
                    b = B[i, y, :, cut]
                    slope_x = minmod(B[ip, y, :, cut] - b, b - B[im, y, :, cut]) * fluid
                    slope_y = minmod(B[i, y + 1, :, cut] - b, b - B[i, y - 1, :, cut]) * fluid
                    ahead = pltpu.roll(b, 7, 0) - b
                    slope_z = minmod(ahead, pltpu.roll(ahead, 1, 0)) * fluid
                    centre = b - HALF * (
                        abs_x[t // 2] * slope_x + xi_y[t % 2] * slope_y + xi_z * slope_z
                    )
                    G[x_at + (y - 1), :, cut] = centre + 0.5 * slope_x
                    if across:
                        if t % 2:
                            G[y_at + y, :, cut] = centre + 0.5 * slope_y
                        else:
                            G[y_at + (y - 1), :, cut] = centre - 0.5 * slope_y
                        edge = centre + jnp.where(up_z, 0.5 * slope_z, -0.5 * slope_z)
                        G[z_at + (y - 1), :, cut] = jnp.where(up_z, edge, pltpu.roll(edge, 7, 0))
            if across:
                for t in range(TILES):
                    cut = slice(t * LANES, (t + 1) * LANES)
                    if t % 2:
                        G[y_at, :, cut] = B[i, 0, :, cut]
                    else:
                        G[y_at + 6, :, cut] = B[i, 7, :, cut]

        upwind(3, True)
        upwind(4, True)
        Sf1[k] = moments(G[0:INNER].reshape(INNER * 8, TILES * LANES))
        start(face_copies(k, 0))

        def total(copies, parts, cut):
            landed(copies)
            tote[:, cut] = parts[k]

        low, high = slice(0, 128), slice(128, 256)

        def no_left():
            tote[:, low] = totc[k, :, low]

        def no_right():
            tote[:, high] = totc[k, :, high]

        pl.when(s > 0)(lambda: total(right_copies(k), Rl, low))
        pl.when(s == 0)(no_left)
        pl.when(s < last)(lambda: total(left_copies(k), Rr, high))
        pl.when(s == last)(no_right)
        target_rows(tote, 256, C, DT, True)
        expansion(C, 256, Le)

        def up_landed():
            landed(near_copies(k))
            landed(far_copies(k))

        pl.when(has_up)(up_landed)
        pl.when(has_down)(lambda: landed(up_copies(k)))

        def no_up():
            F[k, place(0)] = F[k, place(2)]
            F[k, place(1)] = F[k, place(2)]

        def no_down():
            F[k, place(6)] = F[k, place(5)]

        pl.when(jnp.logical_not(has_up))(no_up)
        pl.when(jnp.logical_not(has_down))(no_down)
        for q, (ahead, behind) in ((0, (0, 192)), (1, (64, 128)), (6, (128, 64))):
            at = pl.multiple_of(jnp.where(positive, ahead, behind), 64)
            before(place(q), Le[pl.ds(at, 64), :])
        upwind(1, False)
        upwind(2, True)
        upwind(5, True)
        rest = (FACES - INNER) * 8
        Sf2[k, :, :rest] = moments(G[INNER:FACES].reshape(rest, TILES * LANES))
        start(face_copies(k, 1))

        target = F.at[1, 2:6] if k == 0 else O
        solid_rows(totc.at[k], kr[0:1, :], bound, CM, 256)
        expansion(CM, 256, Lm)
        for p in range(4):
            left = Lm[p * 64 : p * 64 + 64, :].astype(BF16)
            e = jnp.dot(left, TE[...], preferred_element_type=F32)
            a = jnp.dot(left, TA[...], preferred_element_type=F32)
            for t in range(TILES):
                cut = slice(t * LANES, (t + 1) * LANES)
                target[p, :, :, cut] = (a * jnp.exp2(e[:, cut])).reshape(8, 8, LANES)
            W[p] = (4.0 * B[p + 2, 1:7] - F[k, p + 2, 1:7]) * (1.0 / 3.0)

        for g, (sent, got, first, lines, block) in enumerate(
            ((Sf1, Rf1, 0, INNER, 8), (Sf2, Rf2, INNER, FACES - INNER, 10))
        ):
            landed(face_copies(k, g))
            sums = sent[k]
            for d in range(n_vel - 1):
                sums = sums + got[k, d]
            width = sums.shape[1]
            totf[:, :width] = sums
            target_rows(totf, width, C, HALF, False)
            expansion(C, width, Lf)
            size = block * 8
            for j in range(lines // block):
                at = first + j * block

                def get(t, at=at):
                    return G[at : at + block, :, t * LANES : (t + 1) * LANES].reshape(size, LANES)

                def put(t, value, at=at):
                    G[at : at + block, :, t * LANES : (t + 1) * LANES] = value.reshape(
                        block, 8, LANES
                    )

                relax(Lf[j * size : (j + 1) * size, :], get, put)

        for p in (3, 0, 2, 1):
            for y in range(1, 7):
                fluid = kb[p + 1, y] == 1.0
                for t in range(TILES):
                    cut = slice(t * LANES, (t + 1) * LANES)
                    z = G[Z_AT[p] + y - 1, :, cut]
                    change = (
                        xi_x[t // 2]
                        * (G[X_AT[p + 1] + y - 1, :, cut] - G[X_AT[p] + y - 1, :, cut])
                        + xi_y[t % 2] * (G[Y_AT[p] + y, :, cut] - G[Y_AT[p] + y - 1, :, cut])
                        + xi_z * (z - pltpu.roll(z, 1, 0))
                    )
                    fresh = W[p, y - 1, :, cut] - DT * change
                    target[p, y, :, cut] = jnp.where(fluid, fresh, target[p, y, :, cut])
            if k == STEPS - 1:
                pltpu.make_async_copy(O.at[p], out.at[p], out_sem.at[p]).start()
            elif p == 0:
                send_near(k + 1)
            elif p == 1:
                send_far(k + 1)

    one_step(0)
    send_cells(1)
    one_step(1)

    for k in range(STEPS):
        left_free(cell_copies(k))
        pl.when(s < last)(lambda k=k: left_free(right_copies(k)))
        pl.when(s > 0)(lambda k=k: left_free(left_copies(k)))
        pl.when(has_down)(lambda k=k: left_free(near_copies(k) + far_copies(k)))
        pl.when(has_up)(lambda k=k: left_free(up_copies(k)))
        for g in range(2):
            left_free(face_copies(k, g))
    for p in range(4):
        pltpu.make_async_copy(O.at[p], out.at[p], out_sem.at[p]).wait()


def solution(mesh):
    n_space, n_vel = mesh.shape["space"], mesh.shape["vel"]
    vmem, dma = pltpu.VMEM, pltpu.SemaphoreType.DMA
    width = TILES * LANES

    def on_device(dist, cell_type, boundary):
        peers = n_vel - 1
        return pl.pallas_call(
            functools.partial(kernel, n_space, n_vel),
            out_shape=jax.ShapeDtypeStruct(dist.shape, F32),
            in_specs=[
                pl.BlockSpec(memory_space=pltpu.HBM),
                pl.BlockSpec(memory_space=pltpu.HBM),
                pl.BlockSpec(memory_space=pltpu.SMEM),
            ],
            out_specs=pl.BlockSpec(memory_space=pl.ANY),
            scratch_shapes=[
                vmem((2, 8, 8, 8, width), F32),
                vmem((8, 8, 8, width), F32),
                vmem((FACES, 8, width), F32),
                vmem((4, 6, 8, width), F32),
                vmem((4, 8, 8, width), F32),
                vmem((2, 16, 256), F32),
                vmem((2, peers, 16, 256), F32),
                vmem((2, 16, 128), F32),
                vmem((2, 16, 128), F32),
                vmem((2, 16, 256), F32),
                vmem((2, peers, 16, 256), F32),
                vmem((2, 16, 512), F32),
                vmem((2, peers, 16, 512), F32),
                vmem((2, 16, 256), F32),
                vmem((16, 256), F32),
                vmem((16, 512), F32),
                vmem((40, 512), F32),
                vmem((40, 256), F32),
                vmem((256, 128), F32),
                vmem((256, 128), F32),
                vmem((256, 128), F32),
                vmem((512, 128), F32),
                vmem((128, width), BF16),
                vmem((128, width), BF16),
                vmem((128, LANES), BF16),
                vmem((32, width), BF16),
                vmem((8, 8, LANES), jnp.int32),
                vmem((6, 8, 8, LANES), F32),
                vmem((8, 256), F32),
                dma,
                dma,
                dma((4,)),
                dma((2, 3)),
                dma((2, 3)),
                dma((2, peers)),
                dma((2, peers)),
                dma((2,)),
                dma((2,)),
                dma((2,)),
                dma((2,)),
                dma((2, 2, peers)),
                dma((2, 2, peers)),
            ],
            compiler_params=pltpu.CompilerParams(
                collective_id=0, has_side_effects=True, vmem_limit_bytes=60 * 2**20
            ),
        )(dist, jnp.transpose(cell_type, (1, 2, 0)), boundary)

    return jax.shard_map(
        on_device,
        mesh=mesh,
        in_specs=(P("space", None, None, "vel"), P(), P()),
        out_specs=P("space", None, None, "vel"),
        check_vma=False,
    )
```

time: 48.8 us -> 41.7 us (0.85)
  Pallas kernels: 46.9 us -> 39.6 us
    pallas_call x1, Pallas kernels: 46.9 us -> 39.6 us  [on_device(): pl.pallas_call(functools.partial(kernel, n_space, n_vel), out_shape=jax.S...]
    unnamed x6 -> x1, local copies, waits for them, and re-layouts: 1.85 us -> 1.87 us
where the time goes in v1:
time: 41.7 us; the launch traced here: 41.4 us
  Pallas kernels  39.6 us (95%)
  local copies, waits for them, and re-layouts  1.87 us (4%)
    pallas_call x1, Pallas kernels, on_device(): pl.pallas_call(functools.partial(kernel, n_space, n_vel), out_shape=jax.S...  39.6 us
    unnamed x1, local copies, waits for them, and re-layouts  1.87 us

profile of v1, /device:TPU:4, one launch (start us, length us, event | category | flops | bytes accessed | tf_op | source)
XLA Modules:
  0.0 41.4 jit_solution(5772106538479488049)
XLA Ops:
  0.0 39.6 %shard_map.37 = f32[4,8,8,512]{3,2,1,0:T(8,128)} custom-call(f32[4,8,8,512]{3,2,1,0:T(8,128)} %dist.1, s32[8,8,128]{2,1,0:T(8,128)} %bitcast.1, f32[6]{0:T(128)} %bound_ref.1), custom_call_target="tpu_custom_call" | custom-call | tf_op jit(solution)/shard_map/pallas_call | solution.py:588
  39.6 1.9 %copy.5 = f32[4,8,8,512]{3,2,1,0:T(8,128)} copy(f32[4,8,8,512]{3,2,1,0:T(8,128)} %shard_map.37) | data formatting | bytes 1048576

commit v2 on v1

--- a/solution.py
+++ b/solution.py
@@ -24,6 +24,8 @@
 LN_KAPPA2 = 2.0 * math.log(KAPPA)
 TILES = 4
 LANES = 128
+
+FARTHEST_FIRST = (3, 5, 4, 1, 7, 2, 6)
 
 X_AT = (32, 38, 0, 44, 50)
 Y_AT = (56, 6, 13, 63)
@@ -157,7 +159,7 @@
     n_vel,
     dist,
     kinds,
-    bound_ref,
+    bound_any,
     out,
     F,
     B,
@@ -185,11 +187,13 @@
     TP,
     TA,
     T32,
+    bound_ref,
     kt,
     kb,
     kr,
     in_sem,
     kt_sem,
+    bound_sem,
     out_sem,
     halo_s,
     halo_r,
@@ -225,6 +229,8 @@
     load.start()
     kind_load = pltpu.make_async_copy(kinds, kt, kt_sem)
     kind_load.start()
+    bound_load = pltpu.make_async_copy(bound_any, bound_ref, bound_sem)
+    bound_load.start()
 
     node = lax.broadcasted_iota(jnp.int32, (1, TILES * LANES), 1)
     nx = (4 * v - 15 + 2 * (node // 256)).astype(F32)
@@ -275,22 +281,22 @@
             cut = slice(t * LANES, (t + 1) * LANES)
             put(t, a * get(t) + jnp.exp2(e[:, cut]) * p[:, cut])
 
-    def peer_copies(src, dst, send, recv, lo, extra):
+    def peer_copies(src, dst, send, recv):
         return [
             pltpu.make_async_remote_copy(
                 src,
-                dst.at[d - lo],
-                send.at[d - lo],
-                recv.at[d - lo],
-                device_id={**extra, "vel": lax.rem(v + d, n_vel)},
+                dst.at[d - 1],
+                send.at[d - 1],
+                recv.at[d - 1],
+                device_id={"vel": lax.rem(v + d, n_vel)},
                 device_id_type=MESH,
             )
-            for d in range(lo, n_vel)
+            for d in FARTHEST_FIRST
         ]
 
     def cell_copies(k):
         return peer_copies(
-            Sc.at[k], Rc.at[k], cell_s.at[k], cell_r.at[k], 1, {}
+            Sc.at[k], Rc.at[k], cell_s.at[k], cell_r.at[k]
         )
 
     def edge_copies(k, src, dst, send, recv, to):
@@ -365,7 +371,7 @@
     def face_copies(k, g):
         sf, rf = ((Sf1, Rf1), (Sf2, Rf2))[g]
         return peer_copies(
-            sf.at[k], rf.at[k], face_s.at[k, g], face_r.at[k, g], 1, {}
+            sf.at[k], rf.at[k], face_s.at[k, g], face_r.at[k, g]
         )
 
     load.wait()
@@ -379,6 +385,7 @@
     send_far(0)
 
     kind_load.wait()
+    bound_load.wait()
     for j in range(6):
         plane = 4 * s + (j - 1)
         for y in range(8):
@@ -591,7 +598,7 @@
             in_specs=[
                 pl.BlockSpec(memory_space=pltpu.HBM),
                 pl.BlockSpec(memory_space=pltpu.HBM),
-                pl.BlockSpec(memory_space=pltpu.SMEM),
+                pl.BlockSpec(memory_space=pl.ANY),
             ],
             out_specs=pl.BlockSpec(memory_space=pl.ANY),
             scratch_shapes=[
@@ -621,9 +628,11 @@
                 vmem((128, width), BF16),
                 vmem((128, LANES), BF16),
                 vmem((32, width), BF16),
+                pltpu.SMEM((6,), F32),
                 vmem((8, 8, LANES), jnp.int32),
                 vmem((6, 8, 8, LANES), F32),
                 vmem((8, 256), F32),
+                dma,
                 dma,
                 dma,
                 dma((4,)),

time: 41.7 us -> 40.5 us (0.971)
  Pallas kernels: 39.6 us -> 38.5 us
    pallas_call x1, Pallas kernels: 39.6 us -> 38.5 us  [on_device(): pl.pallas_call(functools.partial(kernel, n_space, n_vel), out_shape=jax.S...]
where the time goes in v2:
time: 40.5 us; the launch traced here: 40.4 us
  Pallas kernels  38.5 us (95%)
  local copies, waits for them, and re-layouts  1.87 us (5%)
    pallas_call x1, Pallas kernels, on_device(): pl.pallas_call(functools.partial(kernel, n_space, n_vel), out_shape=jax.S...  38.5 us
    unnamed x1, local copies, waits for them, and re-layouts  1.87 us

profile of v2, /device:TPU:4, one launch (start us, length us, event | category | flops | bytes accessed | tf_op | source)
XLA Modules:
  0.0 40.4 jit_solution(13171345054248161474)
XLA Ops:
  0.0 38.5 %shard_map.37 = f32[4,8,8,512]{3,2,1,0:T(8,128)} custom-call(f32[4,8,8,512]{3,2,1,0:T(8,128)} %dist.1, s32[8,8,128]{2,1,0:T(8,128)} %bitcast.1, f32[6]{0:T(128)} %bound_any.1), custom_call_target="tpu_custom_call" | custom-call | tf_op jit(solution)/shard_map/pallas_call | solution.py:595
  38.5 1.9 %copy.5 = f32[4,8,8,512]{3,2,1,0:T(8,128)} copy(f32[4,8,8,512]{3,2,1,0:T(8,128)} %shard_map.37) | data formatting | bytes 1048576

commit v3 on v2

--- a/solution.py
+++ b/solution.py
@@ -32,6 +32,7 @@
 Z_AT = (70, 20, 26, 76)
 INNER = 32
 FACES = 82
+WIDE = 384
 
 
 def minmod(a, b):
@@ -214,16 +215,15 @@
     place = lambda q: jnp.where(positive, q, 7 - q)
 
     barrier = pltpu.get_barrier_semaphore()
-    for d in range(1, n_vel):
+    def greet(to):
+        pl.semaphore_signal(barrier, 1, device_id={"space": to}, device_id_type=MESH)
+
+    pl.when(s > 0)(lambda: greet(s - 1))
+    pl.when(s < last)(lambda: greet(s + 1))
+    for d in FARTHEST_FIRST:
         pl.semaphore_signal(
             barrier, 1, device_id={"vel": lax.rem(v + d, n_vel)}, device_id_type=MESH
         )
-
-    def greet(to):
-        pl.semaphore_signal(barrier, 1, device_id={"space": to}, device_id_type=MESH)
-
-    pl.when(s > 0)(lambda: greet(s - 1))
-    pl.when(s < last)(lambda: greet(s + 1))
 
     load = pltpu.make_async_copy(dist, F.at[0, 2:6], in_sem)
     load.start()
@@ -507,8 +507,13 @@
         upwind(1, False)
         upwind(2, True)
         upwind(5, True)
-        rest = (FACES - INNER) * 8
-        Sf2[k, :, :rest] = moments(G[INNER:FACES].reshape(rest, TILES * LANES))
+        Sf2[k] = moments(G[INNER : FACES - 2].reshape(WIDE, TILES * LANES))
+        tail = G[FACES - 2 : FACES].reshape(16, TILES * LANES)
+        tail = moments(jnp.concatenate([tail] * 8, axis=0))
+        for h in range(2):
+            Sf2[k, 13 + h : 14 + h, :LANES] = jnp.sum(
+                jnp.where(lane // 16 == (8 - sub) % 8, tail[8 * h : 8 * h + 8], 0.0), axis=0, keepdims=True
+            )
         start(face_copies(k, 1))
 
         target = F.at[1, 2:6] if k == 0 else O
@@ -532,6 +537,13 @@
                 sums = sums + got[k, d]
             width = sums.shape[1]
             totf[:, :width] = sums
+            if g:
+                for h in range(2):
+                    spread = jnp.broadcast_to(sums[13 + h : 14 + h, :LANES], (8, LANES))
+                    totf[8 * h : 8 * h + 8, WIDE:] = pltpu.roll(
+                        spread, 0, 1, stride=16, stride_axis=0
+                    )
+                width = WIDE + LANES
             target_rows(totf, width, C, HALF, False)
             expansion(C, width, Lf)
             size = block * 8
@@ -613,8 +625,8 @@
                 vmem((2, 16, 128), F32),
                 vmem((2, 16, 256), F32),
                 vmem((2, peers, 16, 256), F32),
-                vmem((2, 16, 512), F32),
-                vmem((2, peers, 16, 512), F32),
+                vmem((2, 16, WIDE), F32),
+                vmem((2, peers, 16, WIDE), F32),
                 vmem((2, 16, 256), F32),
                 vmem((16, 256), F32),
                 vmem((16, 512), F32),

time: 40.5 us -> 40.1 us (level)
    pallas_call x1, Pallas kernels: 38.5 us -> 38.1 us  [on_device(): pl.pallas_call(functools.partial(kernel, n_space, n_vel), out_shape=jax.S...]
where the time goes in v3:
time: 40.1 us; the launch traced here: 40 us
  Pallas kernels  38.1 us (95%)
  local copies, waits for them, and re-layouts  1.87 us (5%)
    pallas_call x1, Pallas kernels, on_device(): pl.pallas_call(functools.partial(kernel, n_space, n_vel), out_shape=jax.S...  38.1 us
    unnamed x1, local copies, waits for them, and re-layouts  1.87 us

profile of v3, /device:TPU:4, one launch (start us, length us, event | category | flops | bytes accessed | tf_op | source)
XLA Modules:
  0.0 40.0 jit_solution(16409208981422484969)
XLA Ops:
  0.0 38.1 %shard_map.37 = f32[4,8,8,512]{3,2,1,0:T(8,128)} custom-call(f32[4,8,8,512]{3,2,1,0:T(8,128)} %dist.1, s32[8,8,128]{2,1,0:T(8,128)} %bitcast.1, f32[6]{0:T(128)} %bound_any.1), custom_call_target="tpu_custom_call" | custom-call | tf_op jit(solution)/shard_map/pallas_call | solution.py:607
  38.1 1.9 %copy.5 = f32[4,8,8,512]{3,2,1,0:T(8,128)} copy(f32[4,8,8,512]{3,2,1,0:T(8,128)} %shard_map.37) | data formatting | bytes 1048576
